TPU v7x, 512 devices: a whole 4x4x16 slice. The times are simulated.
512 devices in a mesh: expert: 128 (over z, y, core), dp: 4 (over x).
Axes of the slice: x: 4, y: 4, z: 16, core: 2. Of those that a mesh axis runs over, the one named last changes fastest.
Arguments:
- tokens: bfloat16 [16384, 2048], P('expert', 'dp'), may hold values from -6 to 6
- grad_out: bfloat16 [16384, 2048], P('expert', 'dp'), may hold values from -6 to 6
- routes: int32 [16384, 8], P('expert'), may hold values from 0 to 127, all different within a row; in each aligned block of 128 rows (0 to 127, 128 to 255, ...) at most 12 rows name the same one
- gates: float32 [16384, 8], P('expert'), may hold values from 0.1 to 1
- w_gate: bfloat16 [128, 2048, 384], P('expert', 'dp'), may hold values from -0.125 to 0.125
- w_up: bfloat16 [128, 2048, 384], P('expert', 'dp'), may hold values from -0.125 to 0.125
- w_down: bfloat16 [128, 384, 2048], P('expert', None, 'dp'), may hold values from -0.3125 to 0.3125
Outputs:
- d_tokens: bfloat16 [16384, 2048], P('expert', 'dp')
- grad_gate: bfloat16 [128, 2048, 384], P('expert', 'dp')
- grad_up: bfloat16 [128, 2048, 384], P('expert', 'dp')
- grad_down: bfloat16 [128, 384, 2048], P('expert', None, 'dp')
Inputs may be any that keep to these rules, and one draw needn't show every extreme that they name: `routes`: each row names 8 different experts; in each aligned block of 128 rows no expert is named by more than 12 rows, a bound that some block reaches.
All inputs are finite; a program needn't handle non-finite values.
Results may differ from a plain program's by a relative error of at most 0.013.
Values may be sent and summed in bfloat16 or wider, within the bound.
No kernel may reach another device: no remote copies, remote signals or barrier semaphores. Data moves between devices by JAX's collectives and lax.ppermute only.
A program may use at most 64 MiB of HBM per device.

v0:
```python
import jax
import jax.numpy as jnp
from jax import lax
from jax.sharding import Mesh
from jax.sharding import PartitionSpec as P

MOST = 12
N_Z, N_Y, N_C, N_X = (16, 4, 2, 4)
PLANE = ("x", "y", "c")
F32 = jnp.float32
BF16 = jnp.bfloat16


def dot(left, right, contract, batch=((), ())):
    return lax.dot_general(left, right, (contract, batch), preferred_element_type=F32)


def shift(value, by):
    return lax.ppermute(value, "x", [(i, (i + by) % N_X) for i in range(N_X)])


def gather_x(value, me):
    whole = jnp.zeros((N_X,) + value.shape, value.dtype)
    for by in range(N_X):
        piece = value if by == 0 else shift(value, by)
        whole = lax.dynamic_update_slice_in_dim(whole, piece[None], (me - by) % N_X, 0)
    return whole


def plan(routes, gates, me_z):
    tok = routes.shape[0]
    mine = jnp.concatenate([routes.T.astype(F32), gates.T], axis=0)
    every = lax.all_to_all(
        jnp.broadcast_to(mine[None], (N_Z,) + mine.shape),
        "z",
        split_axis=0,
        concat_axis=0,
        tiled=True,
    )
    top = routes.shape[1]
    near = N_Y * N_C
    named = every[:, :top].reshape(N_Z, top, 1, tok)
    weight = every[:, top:].reshape(N_Z, top, 1, tok)
    wanted = (me_z * near + jnp.arange(near, dtype=jnp.int32)).astype(F32)
    hit = named == wanted[None, None, :, None]
    member = jnp.sum(hit.astype(F32), axis=1)
    gate = jnp.sum(jnp.where(hit, weight, 0.0), axis=1)
    before = (jnp.arange(tok)[:, None] < jnp.arange(tok)[None, :]).astype(BF16)
    rank = dot(member.astype(BF16), before, ((2,), (0,)))
    within = (jnp.arange(N_Z) % (N_Z // N_X) * MOST).astype(F32)
    slot = jnp.where(member > 0.5, rank + within[:, None, None], -1.0)

    def by_group(value):
        value = value.reshape(N_X, N_Z // N_X, near, tok)
        return value.transpose(0, 2, 1, 3).reshape(N_X, near, 1, N_Z // N_X * tok)

    slots = N_Z // N_X * MOST
    pick = by_group(slot) == jnp.arange(slots, dtype=jnp.int32).astype(F32)[None, None, :, None]
    row_gate = jnp.sum(jnp.where(pick, by_group(gate), 0.0), axis=3)
    return (
        pick.astype(BF16).reshape(N_X, near * slots, N_Z // N_X * tok),
        row_gate.reshape(N_X, near * slots, 1),
    )


def shards(tokens, grad_out, routes, gates, w_gate, w_up, w_down):
    me_z, me_x = (lax.axis_index("z"), lax.axis_index("x"))
    tok, cols = tokens.shape
    both = jnp.concatenate([tokens, grad_out], axis=1)
    column = lax.all_gather(both, "z", axis=0, tiled=True).reshape(N_X, N_Z // N_X * tok, 2 * cols)
    pick, row_gate = plan(routes, gates, me_z)
    full_gate = gather_x(w_gate[0], me_x)
    full_up = gather_x(w_up[0], me_x)
    full_down = gather_x(w_down[0], me_x)
    rows = dot(pick, column, ((2,), (1,)), ((0,), (0,)))
    scale = jnp.where(jnp.arange(2 * cols)[None, None, :] < cols, 1.0, row_gate)
    rows = (rows * scale).astype(BF16)
    count = rows.shape[1]
    slots = count // (N_Y * N_C)
    rows = lax.all_to_all(
        rows.reshape(-1, slots, 2 * cols), PLANE, split_axis=0, concat_axis=0, tiled=True
    ).reshape(N_X, count, 2 * cols)
    inputs, scaled = (rows[:, :, :cols], rows[:, :, cols:])

    def over_features(left, right, axis):
        return sum((dot(left[j], right[j], ((1,), (axis,))) for j in range(N_X)))

    pre_gate = over_features(inputs, full_gate, 0)
    pre_up = over_features(inputs, full_up, 0)
    back_hidden = over_features(scaled, full_down, 1)
    sigmoid_gate = jax.nn.sigmoid(pre_gate)
    activated = pre_gate * sigmoid_gate
    hidden = (activated * pre_up).astype(BF16)
    d_up = (back_hidden * activated).astype(BF16)
    d_gate = (back_hidden * pre_up * sigmoid_gate * (1.0 + pre_gate * (1.0 - sigmoid_gate))).astype(
        BF16
    )
    row_grad = jnp.stack(
        [
            (dot(d_gate, full_gate[j], ((1,), (1,))) + dot(d_up, full_up[j], ((1,), (1,)))).astype(
                BF16
            )
            for j in range(N_X)
        ]
    )
    came_back = lax.all_to_all(
        row_grad.reshape(-1, slots, cols), PLANE, split_axis=0, concat_axis=0, tiled=True
    ).reshape(N_X, count, cols)
    token_grad = dot(pick, came_back, ((1,), (1,)), ((0,), (0,))).astype(BF16)
    d_tokens = lax.psum_scatter(token_grad.reshape(-1, cols), "z", scatter_dimension=0, tiled=True)
    totals = [None, None, None]
    for by in (1, 3, 2, 0):
        to = (me_x + by) % N_X
        ins = lax.dynamic_index_in_dim(inputs, to, 0, keepdims=False)
        outs = lax.dynamic_index_in_dim(scaled, to, 0, keepdims=False)
        for k, (left, right) in enumerate(((ins, d_gate), (ins, d_up), (hidden, outs))):
            part = dot(left, right, ((0,), (0,))).astype(BF16)
            part = (shift(part, by) if by else part).astype(F32)
            totals[k] = part if totals[k] is None else totals[k] + part
    grads = [total.astype(BF16)[None] for total in totals]
    return (d_tokens, *grads)


def solution(mesh):
    fine = Mesh(mesh.devices.reshape(N_Z, N_Y, N_C, N_X), ("z", "y", "c", "x"))
    expert = ("z", "y", "c")
    return jax.shard_map(
        shards,
        mesh=fine,
        in_specs=(
            P(expert, "x"),
            P(expert, "x"),
            P(expert, None),
            P(expert, None),
            P(expert, "x", None),
            P(expert, "x", None),
            P(expert, None, "x"),
        ),
        out_specs=(
            P(expert, "x"),
            P(expert, "x", None),
            P(expert, "x", None),
            P(expert, None, "x"),
        ),
        check_vma=False,
    )
```

profile of v0, /device:TPU:4, one launch (start us, length us, event | category | flops | bytes accessed | tf_op | source)
XLA Modules:
  0.0 332.0 jit_solution(9735553200323661937)
XLA Ops:
  7.2 1.7 pad_maximum_fusion.1
  11.0 15.2 %all-to-all-start = ((f32[16,16,128]{2,1,0:T(8,128)}), f32[16,16,128]{2,1,0:T(8,128)S(1)}, u32[]{:S(2)}, u32[]{:S(2)}) async-start(f32[16,16,128]{2,1,0:T(8,128)} %broadcast_in_dim.103), calls=%async_computation | async-start | bytes 262144 | tf_op jit(solution)/shard_map/all_to_all | solution.py:33
  26.3 14.6 %all-to-all-done = f32[16,16,128]{2,1,0:T(8,128)S(1)} async-done(((f32[16,16,128]{2,1,0:T(8,128)}), f32[16,16,128]{2,1,0:T(8,128)S(1)}, u32[]{:S(2)}, u32[]{:S(2)}) %all-to-all-start) | async-done | bytes 131104 | tf_op jit(solution)/shard_map/all_to_all | solution.py:33
  42.3 52.2 %all-gather.2.cloned.1.call-done = bf16[2048,1024]{1,0:T(8,128)(2,1)} async-done(((bf16[128,1024]{1,0:T(8,128)(2,1)}), bf16[2048,1024]{1,0:T(8,128)(2,1)}) %all-gather.2.cloned.1.call-update) | async-done | bytes 4194320 | tf_op jit(solution)/shard_map/all_gather | solution.py:70
  94.4 5.6 %multiply_convert_fusion = bf16[4,384,1024]{2,1,0:T(8,128)(2,1)} fusion(f32[4,384]{1,0:T(4,128)S(1)} %broadcast_in_dim.112, pred[1024]{0:T(1024)(128)(4,1)S(1)} %iota_compare_fusion.1, pred[4,384,512]{2,1,0:T(32,128)(4,1)S(1)} %bitcast_compare_fusion, bf16[4,512,1024]{2,1,0:T(8,128)(2,1)} %bitcast.227), kind=kOutput, calls=%fused_computation | convolution fusion | flops 1615331328 | bytes 8133632 | tf_op jit(solution)/shard_map/dot_general | solution.py:15
  100.1 7.6 %all-to-all-start.1 = ((bf16[32,48,1024]{2,1,0:T(8,128)(2,1)}), bf16[32,48,1024]{2,1,0:T(8,128)(2,1)S(1)}, u32[]{:S(2)}, u32[]{:S(2)}) async-start(bf16[32,48,1024]{2,1,0:T(8,128)(2,1)} %bitcast.213), calls=%async_computation.1 | async-start | bytes 6291456 | tf_op jit(solution)/shard_map/all_to_all | solution.py:80
  107.7 3.1 collective-permute-start.6
  110.9 2.7 collective-permute-start.7
  113.6 2.7 collective-permute-start.8
  116.3 3.2 collective-permute-start
  119.5 4.6 %collective-permute-start.1 = (bf16[384,512]{1,0:T(8,128)(2,1)}, bf16[384,512]{1,0:T(8,128)(2,1)}, u32[]{:S(2)}, u32[]{:S(2)}) collective-permute-start(bf16[384,512]{1,0:T(8,128)(2,1)} %bitcast.220), channel_id=1, source_target_pairs={{0,2},{1,3},{2,0},{3,1},{4,6},{5,7},{6,4},{7,5},{8,10},{9,11},{10,... | collective-permute-start | bytes 1179656 | tf_op jit(solution)/shard_map/ppermute | solution.py:19
  130.5 22.3 %collective-permute-done.6 = bf16[512,384]{1,0:T(8,128)(2,1)} collective-permute-done((bf16[512,384]{1,0:T(8,128)(2,1)S(1)}, bf16[512,384]{1,0:T(8,128)(2,1)}, u32[]{:S(2)}, u32[]{:S(2)}) %collective-permute-start.6) | collective-permute-done | bytes 393248 | tf_op jit(solution)/shard_map/ppermute | solution.py:19
  152.8 2.7 collective-permute-start.2
  155.5 1.8 bitcast_dynamic-update-slice_fusion.2
  157.3 12.5 %collective-permute-done = bf16[384,512]{1,0:T(8,128)(2,1)} collective-permute-done((bf16[384,512]{1,0:T(8,128)(2,1)}, bf16[384,512]{1,0:T(8,128)(2,1)}, u32[]{:S(2)}, u32[]{:S(2)}) %collective-permute-start) | collective-permute-done | bytes 393248 | tf_op jit(solution)/shard_map/ppermute | solution.py:19
  169.8 4.4 %collective-permute-start.3 = (bf16[512,384]{1,0:T(8,128)(2,1)S(1)}, bf16[512,384]{1,0:T(8,128)(2,1)S(1)}, u32[]{:S(2)}, u32[]{:S(2)}) collective-permute-start(bf16[512,384]{1,0:T(8,128)(2,1)S(1)} %bitcast.222), channel_id=1, source_target_pairs={{0,1},{1,2},{2,3},{3,0},{4,5},{5,6},{6,7},{7,4},{8,9},{9,10},{10,1... | collective-permute-start | bytes 1179656 | tf_op jit(solution)/shard_map/ppermute | solution.py:19
  174.2 1.8 bitcast_dynamic-update-slice_fusion.8
  176.0 1.9 collective-permute-start.4
  177.9 1.8 bitcast_dynamic-update-slice_fusion.1
  179.7 3.4 %collective-permute-start.5 = (bf16[512,384]{1,0:T(8,128)(2,1)S(1)}, bf16[512,384]{1,0:T(8,128)(2,1)S(1)}, u32[]{:S(2)}, u32[]{:S(2)}) collective-permute-start(bf16[512,384]{1,0:T(8,128)(2,1)S(1)} %bitcast.224), channel_id=1, source_target_pairs={{0,3},{1,0},{2,1},{3,2},{4,7},{5,4},{6,5},{7,6},{8,11},{9,8},{10,9... | collective-permute-start | bytes 1179656 | tf_op jit(solution)/shard_map/ppermute | solution.py:19
  183.1 1.8 bitcast_dynamic-update-slice_fusion.7
  184.9 1.8 bitcast_dynamic-update-slice_fusion
  188.2 6.6 %collective-permute-done.4 = bf16[512,384]{1,0:T(8,128)(2,1)S(1)} collective-permute-done((bf16[512,384]{1,0:T(8,128)(2,1)S(1)}, bf16[512,384]{1,0:T(8,128)(2,1)S(1)}, u32[]{:S(2)}, u32[]{:S(2)}) %collective-permute-start.4) | collective-permute-done | bytes 393248 | tf_op jit(solution)/shard_map/ppermute | solution.py:19
  203.5 1.4 convolution_add_fusion.12
  206.3 1.4 convolution_add_fusion.10
  211.8 2.3 multiply_convert_fusion.1
  214.0 1.5 fusion.46
  215.5 1.4 fusion.45
  216.9 1.4 fusion.44
  218.3 1.4 fusion.41
  219.7 1.4 fusion.7
  221.1 1.4 fusion.8
  222.5 1.4 fusion.9
  224.0 1.4 fusion.10
  225.6 29.2 %all_to_all.15 = bf16[32,48,512]{2,1,0:T(8,128)(2,1)S(1)} all-to-all(bf16[32,48,512]{2,1,0:T(8,128)(2,1)S(1)} %bitcast.211), channel_id=1, replica_groups=mesh['z'=16,'y'=4,'c'=2,'x'=4] {'x','y','c'}, dimensions={0} | all-to-all | bytes 3145728 | tf_op jit(solution)/shard_map/all_to_all | solution.py:106
  254.7 2.6 convolution_convert_fusion
  258.2 3.7 %collective-permute-start.11 = (bf16[512,384]{1,0:T(8,128)(2,1)S(1)}, bf16[512,384]{1,0:T(8,128)(2,1)S(1)}, u32[]{:S(2)}, u32[]{:S(2)}) collective-permute-start(bf16[512,384]{1,0:T(8,128)(2,1)S(1)} %convolution_convert_fusion.10), channel_id=1, source_target_pairs={{0,2},{1,3},{2,0},{3,1},{4,6},{5,7},{6,4},{7,5},{8,10},{9,11},{10,... | collective-permute-start | bytes 1179656 | tf_op jit(solution)/shard_map/ppermute | solution.py:19
  262.4 2.5 collective-permute-start.10
  265.3 4.5 %collective-permute-start.17 = (bf16[384,512]{1,0:T(8,128)(2,1)S(1)}, bf16[384,512]{1,0:T(8,128)(2,1)S(1)}, u32[]{:S(2)}, u32[]{:S(2)}) collective-permute-start(bf16[384,512]{1,0:T(8,128)(2,1)S(1)} %convolution_convert_fusion.2), channel_id=1, source_target_pairs={{0,2},{1,3},{2,0},{3,1},{4,6},{5,7},{6,4},{7,5},{8,10},{9,11},{10,... | collective-permute-start | bytes 1179656 | tf_op jit(solution)/shard_map/ppermute | solution.py:19
  270.2 2.4 collective-permute-start.16
  273.0 3.5 %collective-permute-start.15 = (bf16[384,512]{1,0:T(8,128)(2,1)S(1)}, bf16[384,512]{1,0:T(8,128)(2,1)S(1)}, u32[]{:S(2)}, u32[]{:S(2)}) collective-permute-start(bf16[384,512]{1,0:T(8,128)(2,1)S(1)} %convolution_convert_fusion.4), channel_id=1, source_target_pairs={{0,1},{1,2},{2,3},{3,0},{4,5},{5,6},{6,7},{7,4},{8,9},{9,10},{10,1... | collective-permute-start | bytes 1179656 | tf_op jit(solution)/shard_map/ppermute | solution.py:19
  277.8 4.4 %collective-permute-start.9 = (bf16[512,384]{1,0:T(8,128)(2,1)S(1)}, bf16[512,384]{1,0:T(8,128)(2,1)S(1)}, u32[]{:S(2)}, u32[]{:S(2)}) collective-permute-start(bf16[512,384]{1,0:T(8,128)(2,1)S(1)} %convolution_convert_fusion.12), channel_id=1, source_target_pairs={{0,1},{1,2},{2,3},{3,0},{4,5},{5,6},{6,7},{7,4},{8,9},{9,10},{10,1... | collective-permute-start | bytes 1179656 | tf_op jit(solution)/shard_map/ppermute | solution.py:19
  282.8 3.0 collective-permute-start.14
  285.8 12.4 %collective-permute-done.16 = bf16[384,512]{1,0:T(8,128)(2,1)S(1)} collective-permute-done((bf16[384,512]{1,0:T(8,128)(2,1)S(1)}, bf16[384,512]{1,0:T(8,128)(2,1)S(1)}, u32[]{:S(2)}, u32[]{:S(2)}) %collective-permute-start.16) | collective-permute-done | bytes 393248 | tf_op jit(solution)/shard_map/ppermute | solution.py:19
  298.2 3.2 collective-permute-start.13
  301.4 2.6 collective-permute-start.12
  307.2 7.7 %collective-permute-done.13 = bf16[512,384]{1,0:T(8,128)(2,1)S(1)} collective-permute-done((bf16[512,384]{1,0:T(8,128)(2,1)S(1)}, bf16[512,384]{1,0:T(8,128)(2,1)S(1)}, u32[]{:S(2)}, u32[]{:S(2)}) %collective-permute-start.13) | collective-permute-done | bytes 393248 | tf_op jit(solution)/shard_map/ppermute | solution.py:19
  316.4 8.7 %reduce-scatter.2.cloned.1.call-done = bf16[128,512]{1,0:T(8,128)(2,1)} async-done(((bf16[2048,512]{1,0:T(8,128)(2,1)}), bf16[128,512]{1,0:T(8,128)(2,1)}) %reduce-scatter.2.cloned.1.call-update) | async-done | bytes 131088 | tf_op jit(solution)/shard_map/reduce_scatter | solution.py:110
  (84 shorter events, 34.7 us)
Async XLA Ops:
  7.2 87.3 %all-gather.2.cloned.1.call-start = ((), (), s32[]{:S(2)}) async-start(), calls=%async_computation.4 | async-start | bytes 4456448 | tf_op jit(solution)/shard_map/all_gather | solution.py:70
  11.0 29.9 %all-to-all-start = ((f32[16,16,128]{2,1,0:T(8,128)}), f32[16,16,128]{2,1,0:T(8,128)S(1)}, u32[]{:S(2)}, u32[]{:S(2)}) async-start(f32[16,16,128]{2,1,0:T(8,128)} %broadcast_in_dim.103), calls=%async_computation | async-start | bytes 262144 | tf_op jit(solution)/shard_map/all_to_all | solution.py:33
  41.7 58.3 %copy-start.3 = (pred[4,384,512]{2,1,0:T(32,128)(4,1)}, pred[4,384,512]{2,1,0:T(32,128)(4,1)S(1)}, u32[]{:S(2)}) copy-start(pred[4,384,512]{2,1,0:T(32,128)(4,1)S(1)} %bitcast_compare_fusion) | copy-start | bytes 2359300
  100.1 7.7 %copy-start.5 = (bf16[1,512,384]{2,1,0:T(8,128)(2,1)S(1)}, bf16[1,512,384]{2,1,0:T(8,128)(2,1)}, u32[]{:S(2)}) copy-start(bf16[1,512,384]{2,1,0:T(8,128)(2,1)} %param.11) | copy-start | bytes 1179652
  100.1 96.6 %all-to-all-start.1 = ((bf16[32,48,1024]{2,1,0:T(8,128)(2,1)}), bf16[32,48,1024]{2,1,0:T(8,128)(2,1)S(1)}, u32[]{:S(2)}, u32[]{:S(2)}) async-start(bf16[32,48,1024]{2,1,0:T(8,128)(2,1)} %bitcast.213), calls=%async_computation.1 | async-start | bytes 6291456 | tf_op jit(solution)/shard_map/all_to_all | solution.py:80
  107.7 217.5 %reduce-scatter.2.cloned.1.call-start = ((), (), s32[]{:S(2)}) async-start(), calls=%async_computation.5 | async-start | bytes 2228224 | tf_op jit(solution)/shard_map/reduce_scatter | solution.py:110
  107.7 45.1 %collective-permute-start.6 = (bf16[512,384]{1,0:T(8,128)(2,1)S(1)}, bf16[512,384]{1,0:T(8,128)(2,1)}, u32[]{:S(2)}, u32[]{:S(2)}) collective-permute-start(bf16[512,384]{1,0:T(8,128)(2,1)S(1)} %bitcast.216), channel_id=1, source_target_pairs={{0,1},{1,2},{2,3},{3,0},{4,5},{5,6},{6,7},{7,4},{8,9},{9,10},{10,1... | collective-permute-start | bytes 1179656 | tf_op jit(solution)/shard_map/ppermute | solution.py:19
  110.9 65.1 %collective-permute-start.7 = (bf16[512,384]{1,0:T(8,128)(2,1)S(1)}, bf16[512,384]{1,0:T(8,128)(2,1)}, u32[]{:S(2)}, u32[]{:S(2)}) collective-permute-start(bf16[512,384]{1,0:T(8,128)(2,1)S(1)} %bitcast.217), channel_id=1, source_target_pairs={{0,2},{1,3},{2,0},{3,1},{4,6},{5,7},{6,4},{7,5},{8,10},{9,11},{10,... | collective-permute-start | bytes 1179656 | tf_op jit(solution)/shard_map/ppermute | solution.py:19
  113.6 71.3 %collective-permute-start.8 = (bf16[512,384]{1,0:T(8,128)(2,1)S(1)}, bf16[512,384]{1,0:T(8,128)(2,1)}, u32[]{:S(2)}, u32[]{:S(2)}) collective-permute-start(bf16[512,384]{1,0:T(8,128)(2,1)S(1)} %bitcast.218), channel_id=1, source_target_pairs={{0,3},{1,0},{2,1},{3,2},{4,7},{5,4},{6,5},{7,6},{8,11},{9,8},{10,9... | collective-permute-start | bytes 1179656 | tf_op jit(solution)/shard_map/ppermute | solution.py:19
  116.3 53.5 %collective-permute-start = (bf16[384,512]{1,0:T(8,128)(2,1)}, bf16[384,512]{1,0:T(8,128)(2,1)}, u32[]{:S(2)}, u32[]{:S(2)}) collective-permute-start(bf16[384,512]{1,0:T(8,128)(2,1)} %bitcast.219), channel_id=1, source_target_pairs={{0,1},{1,2},{2,3},{3,0},{4,5},{5,6},{6,7},{7,4},{8,9},{9,10},{10,1... | collective-permute-start | bytes 1179656 | tf_op jit(solution)/shard_map/ppermute | solution.py:19
  119.5 60.2 %collective-permute-start.1 = (bf16[384,512]{1,0:T(8,128)(2,1)}, bf16[384,512]{1,0:T(8,128)(2,1)}, u32[]{:S(2)}, u32[]{:S(2)}) collective-permute-start(bf16[384,512]{1,0:T(8,128)(2,1)} %bitcast.220), channel_id=1, source_target_pairs={{0,2},{1,3},{2,0},{3,1},{4,6},{5,7},{6,4},{7,5},{8,10},{9,11},{10,... | collective-permute-start | bytes 1179656 | tf_op jit(solution)/shard_map/ppermute | solution.py:19
  125.4 2.1 copy-start.6
  128.3 1.4 copy-start.8
  128.3 24.5 %copy-start.7 = (bf16[1,384,512]{2,1,0:T(8,128)(2,1)S(1)}, bf16[1,384,512]{2,1,0:T(8,128)(2,1)}, u32[]{:S(2)}) copy-start(bf16[1,384,512]{2,1,0:T(8,128)(2,1)} %param.13) | copy-start | bytes 1179652
  152.8 33.8 %collective-permute-start.2 = (bf16[384,512]{1,0:T(8,128)(2,1)S(1)}, bf16[384,512]{1,0:T(8,128)(2,1)S(1)}, u32[]{:S(2)}, u32[]{:S(2)}) collective-permute-start(bf16[384,512]{1,0:T(8,128)(2,1)S(1)} %bitcast.221), channel_id=1, source_target_pairs={{0,3},{1,0},{2,1},{3,2},{4,7},{5,4},{6,5},{7,6},{8,11},{9,8},{10,9... | collective-permute-start | bytes 1179656 | tf_op jit(solution)/shard_map/ppermute | solution.py:19
  169.8 17.6 %collective-permute-start.3 = (bf16[512,384]{1,0:T(8,128)(2,1)S(1)}, bf16[512,384]{1,0:T(8,128)(2,1)S(1)}, u32[]{:S(2)}, u32[]{:S(2)}) collective-permute-start(bf16[512,384]{1,0:T(8,128)(2,1)S(1)} %bitcast.222), channel_id=1, source_target_pairs={{0,1},{1,2},{2,3},{3,0},{4,5},{5,6},{6,7},{7,4},{8,9},{9,10},{10,1... | collective-permute-start | bytes 1179656 | tf_op jit(solution)/shard_map/ppermute | solution.py:19
  176.0 18.9 %collective-permute-start.4 = (bf16[512,384]{1,0:T(8,128)(2,1)S(1)}, bf16[512,384]{1,0:T(8,128)(2,1)S(1)}, u32[]{:S(2)}, u32[]{:S(2)}) collective-permute-start(bf16[512,384]{1,0:T(8,128)(2,1)S(1)} %bitcast.223), channel_id=1, source_target_pairs={{0,2},{1,3},{2,0},{3,1},{4,6},{5,7},{6,4},{7,5},{8,10},{9,11},{10,... | collective-permute-start | bytes 1179656 | tf_op jit(solution)/shard_map/ppermute | solution.py:19
  179.7 16.1 %collective-permute-start.5 = (bf16[512,384]{1,0:T(8,128)(2,1)S(1)}, bf16[512,384]{1,0:T(8,128)(2,1)S(1)}, u32[]{:S(2)}, u32[]{:S(2)}) collective-permute-start(bf16[512,384]{1,0:T(8,128)(2,1)S(1)} %bitcast.224), channel_id=1, source_target_pairs={{0,3},{1,0},{2,1},{3,2},{4,7},{5,4},{6,5},{7,6},{8,11},{9,8},{10,9... | collective-permute-start | bytes 1179656 | tf_op jit(solution)/shard_map/ppermute | solution.py:19
  214.0 4.3 %copy-start = (bf16[384,384]{1,0:T(8,128)(2,1)}, bf16[384,384]{1,0:T(8,128)(2,1)S(1)}, u32[]{:S(2)}) copy-start(bf16[384,384]{1,0:T(8,128)(2,1)S(1)} %get-tuple-element.10) | copy-start | bytes 884740
  225.6 29.2 %copy-start.4 = (pred[4,384,512]{2,1,0:T(32,128)(4,1)S(1)}, pred[4,384,512]{2,1,0:T(32,128)(4,1)}, u32[]{:S(2)}) copy-start(pred[4,384,512]{2,1,0:T(32,128)(4,1)} %copy-done.3) | copy-start | bytes 2359300
  257.7 7.2 %copy-start.2 = (bf16[384,384]{1,0:T(8,128)(2,1)S(1)}, bf16[384,384]{1,0:T(8,128)(2,1)}, u32[]{:S(2)}) copy-start(bf16[384,384]{1,0:T(8,128)(2,1)} %get-tuple-element.8) | copy-start | bytes 884740
  258.2 19.7 %collective-permute-start.11 = (bf16[512,384]{1,0:T(8,128)(2,1)S(1)}, bf16[512,384]{1,0:T(8,128)(2,1)S(1)}, u32[]{:S(2)}, u32[]{:S(2)}) collective-permute-start(bf16[512,384]{1,0:T(8,128)(2,1)S(1)} %convolution_convert_fusion.10), channel_id=1, source_target_pairs={{0,2},{1,3},{2,0},{3,1},{4,6},{5,7},{6,4},{7,5},{8,10},{9,11},{10,... | collective-permute-start | bytes 1179656 | tf_op jit(solution)/shard_map/ppermute | solution.py:19
  262.4 42.8 %collective-permute-start.10 = (bf16[512,384]{1,0:T(8,128)(2,1)S(1)}, bf16[512,384]{1,0:T(8,128)(2,1)S(1)}, u32[]{:S(2)}, u32[]{:S(2)}) collective-permute-start(bf16[512,384]{1,0:T(8,128)(2,1)S(1)} %convolution_convert_fusion.11), channel_id=1, source_target_pairs={{0,3},{1,0},{2,1},{3,2},{4,7},{5,4},{6,5},{7,6},{8,11},{9,8},{10,9... | collective-permute-start | bytes 1179656 | tf_op jit(solution)/shard_map/ppermute | solution.py:19
  265.3 11.6 %copy-start.1 = (bf16[384,384]{1,0:T(8,128)(2,1)S(1)}, bf16[384,384]{1,0:T(8,128)(2,1)}, u32[]{:S(2)}) copy-start(bf16[384,384]{1,0:T(8,128)(2,1)} %copy-done) | copy-start | bytes 884740
  265.3 17.5 %collective-permute-start.17 = (bf16[384,512]{1,0:T(8,128)(2,1)S(1)}, bf16[384,512]{1,0:T(8,128)(2,1)S(1)}, u32[]{:S(2)}, u32[]{:S(2)}) collective-permute-start(bf16[384,512]{1,0:T(8,128)(2,1)S(1)} %convolution_convert_fusion.2), channel_id=1, source_target_pairs={{0,2},{1,3},{2,0},{3,1},{4,6},{5,7},{6,4},{7,5},{8,10},{9,11},{10,... | collective-permute-start | bytes 1179656 | tf_op jit(solution)/shard_map/ppermute | solution.py:19
  270.2 28.0 %collective-permute-start.16 = (bf16[384,512]{1,0:T(8,128)(2,1)S(1)}, bf16[384,512]{1,0:T(8,128)(2,1)S(1)}, u32[]{:S(2)}, u32[]{:S(2)}) collective-permute-start(bf16[384,512]{1,0:T(8,128)(2,1)S(1)} %convolution_convert_fusion.3), channel_id=1, source_target_pairs={{0,3},{1,0},{2,1},{3,2},{4,7},{5,4},{6,5},{7,6},{8,11},{9,8},{10,9... | collective-permute-start | bytes 1179656 | tf_op jit(solution)/shard_map/ppermute | solution.py:19
  273.0 28.4 %collective-permute-start.15 = (bf16[384,512]{1,0:T(8,128)(2,1)S(1)}, bf16[384,512]{1,0:T(8,128)(2,1)S(1)}, u32[]{:S(2)}, u32[]{:S(2)}) collective-permute-start(bf16[384,512]{1,0:T(8,128)(2,1)S(1)} %convolution_convert_fusion.4), channel_id=1, source_target_pairs={{0,1},{1,2},{2,3},{3,0},{4,5},{5,6},{6,7},{7,4},{8,9},{9,10},{10,1... | collective-permute-start | bytes 1179656 | tf_op jit(solution)/shard_map/ppermute | solution.py:19
  277.8 27.3 %collective-permute-start.9 = (bf16[512,384]{1,0:T(8,128)(2,1)S(1)}, bf16[512,384]{1,0:T(8,128)(2,1)S(1)}, u32[]{:S(2)}, u32[]{:S(2)}) collective-permute-start(bf16[512,384]{1,0:T(8,128)(2,1)S(1)} %convolution_convert_fusion.12), channel_id=1, source_target_pairs={{0,1},{1,2},{2,3},{3,0},{4,5},{5,6},{6,7},{7,4},{8,9},{9,10},{10,1... | collective-permute-start | bytes 1179656 | tf_op jit(solution)/shard_map/ppermute | solution.py:19
  282.8 24.5 %collective-permute-start.14 = (bf16[512,384]{1,0:T(8,128)(2,1)S(1)}, bf16[512,384]{1,0:T(8,128)(2,1)S(1)}, u32[]{:S(2)}, u32[]{:S(2)}) collective-permute-start(bf16[512,384]{1,0:T(8,128)(2,1)S(1)} %convolution_convert_fusion.6), channel_id=1, source_target_pairs={{0,2},{1,3},{2,0},{3,1},{4,6},{5,7},{6,4},{7,5},{8,10},{9,11},{10,... | collective-permute-start | bytes 1179656 | tf_op jit(solution)/shard_map/ppermute | solution.py:19
  298.2 16.7 %collective-permute-start.13 = (bf16[512,384]{1,0:T(8,128)(2,1)S(1)}, bf16[512,384]{1,0:T(8,128)(2,1)S(1)}, u32[]{:S(2)}, u32[]{:S(2)}) collective-permute-start(bf16[512,384]{1,0:T(8,128)(2,1)S(1)} %convolution_convert_fusion.7), channel_id=1, source_target_pairs={{0,3},{1,0},{2,1},{3,2},{4,7},{5,4},{6,5},{7,6},{8,11},{9,8},{10,9... | collective-permute-start | bytes 1179656 | tf_op jit(solution)/shard_map/ppermute | solution.py:19
  301.4 13.8 %collective-permute-start.12 = (bf16[512,384]{1,0:T(8,128)(2,1)S(1)}, bf16[512,384]{1,0:T(8,128)(2,1)S(1)}, u32[]{:S(2)}, u32[]{:S(2)}) collective-permute-start(bf16[512,384]{1,0:T(8,128)(2,1)S(1)} %convolution_convert_fusion.8), channel_id=1, source_target_pairs={{0,1},{1,2},{2,3},{3,0},{4,5},{5,6},{6,7},{7,4},{8,9},{9,10},{10,1... | collective-permute-start | bytes 1179656 | tf_op jit(solution)/shard_map/ppermute | solution.py:19
Sparse Core Ops, SparseCore 0:
  10.7 83.7 all-gather.1
  257.5 67.6 reduce-scatter.1
where the time goes:
time: 334 us; the launch traced here: 332 us
  waiting for transfers between devices  138 us (41%)
  starting transfers between devices  81.4 us (24%)
  matrix products  44.4 us (13%)
  blocking collectives  29.2 us (9%)
  local copies, waits for them, and re-layouts  19.6 us (6%)
  between operations  14.7 us (4%)
  other arithmetic  4.4 us (1%)
    ppermute x18, waiting for transfers between devices, shift(): return lax.ppermute(value, 'x', [(i, (i + by) % N_X) for i in range(N_X)])  62.9 us
    ppermute x18, starting transfers between devices, shift(): return lax.ppermute(value, 'x', [(i, (i + by) % N_X) for i in range(N_X)])  58.5 us
    all_gather x1, waiting for transfers between devices, shards(): lax.all_gather(both, 'z', axis=0, tiled=True)  52.2 us
    dot_general x35, matrix products, dot(): lax.dot_general(left, right, (contract, batch), preferred_element_type=F32)  44.4 us
    all_to_all x1, blocking collectives, shards(): lax.all_to_all(row_grad.reshape(-1, slots, cols), PLANE, split_axis=0, co...  29.2 us
    all_to_all x1, starting transfers between devices, plan(): lax.all_to_all(jnp.broadcast_to(mine[None], (N_Z,) + mine.shape), 'z', sp...  15.2 us
    all_to_all x1, waiting for transfers between devices, plan(): lax.all_to_all(jnp.broadcast_to(mine[None], (N_Z,) + mine.shape), 'z', sp...  14.6 us
    dynamic_update_slice x12, local copies, waits for them, and re-layouts, gather_x(): lax.dynamic_update_slice_in_dim(whole, piece[None], (me - by) % N_X, 0)  14.5 us
  transfers between devices with their start and end apart: 22, of which 11 were waited for; matrix products, arithmetic and copies ran while one was open for 9% of the time, Pallas kernels for 0%

commit v1 on v0

--- a/solution.py
+++ b/solution.py
@@ -67,7 +67,9 @@
     me_z, me_x = (lax.axis_index("z"), lax.axis_index("x"))
     tok, cols = tokens.shape
     both = jnp.concatenate([tokens, grad_out], axis=1)
-    column = lax.all_gather(both, "z", axis=0, tiled=True).reshape(N_X, N_Z // N_X * tok, 2 * cols)
+    column = jnp.concatenate(
+        lax.all_to_all(jnp.stack([both] * lax.axis_size("z")), "z", 0, 0), axis=0
+    ).reshape(N_X, N_Z // N_X * tok, 2 * cols)
     pick, row_gate = plan(routes, gates, me_z)
     full_gate = gather_x(w_gate[0], me_x)
     full_up = gather_x(w_up[0], me_x)

time: 334 us -> 471 us (1.41)
  the two profiles are of different devices: /device:TPU:4 before, /device:TPU:8 now
where the time goes in v1:
time: 471 us; the launch traced here: 469 us
  waiting for transfers between devices  269 us (57%)
  starting transfers between devices  87.9 us (19%)
  matrix products  44.5 us (9%)
  blocking collectives  26.9 us (6%)
  local copies, waits for them, and re-layouts  22.2 us (5%)
  between operations  14.7 us (3%)
    all_to_all x1, waiting for transfers between devices, shards(): lax.all_to_all(jnp.stack([both] * lax.axis_size('z')), 'z', 0, 0)  180 us
    ppermute x18, waiting for transfers between devices, shift(): return lax.ppermute(value, 'x', [(i, (i + by) % N_X) for i in range(N_X)])  64.1 us
    ppermute x18, starting transfers between devices, shift(): return lax.ppermute(value, 'x', [(i, (i + by) % N_X) for i in range(N_X)])  60.4 us
    dot_general x35, matrix products, dot(): lax.dot_general(left, right, (contract, batch), preferred_element_type=F32)  44.5 us
    all_to_all x1, blocking collectives, shards(): lax.all_to_all(row_grad.reshape(-1, slots, cols), PLANE, split_axis=0, co...  26.9 us
    all_to_all x1, starting transfers between devices, plan(): lax.all_to_all(jnp.broadcast_to(mine[None], (N_Z,) + mine.shape), 'z', sp...  15.2 us
    dynamic_update_slice x12, local copies, waits for them, and re-layouts, gather_x(): lax.dynamic_update_slice_in_dim(whole, piece[None], (me - by) % N_X, 0)  14.6 us
    all_to_all x1, waiting for transfers between devices, plan(): lax.all_to_all(jnp.broadcast_to(mine[None], (N_Z,) + mine.shape), 'z', sp...  13.7 us
  transfers between devices with their start and end apart: 22, of which 12 were waited for; matrix products, arithmetic and copies ran while one was open for 6% of the time, Pallas kernels for 0%

profile of v1, /device:TPU:8, one launch (start us, length us, event | category | flops | bytes accessed | tf_op | source)
XLA Modules:
  0.0 468.5 jit_solution(3113845418202620086)
XLA Ops:
  9.2 15.2 %all-to-all-start = ((f32[16,16,128]{2,1,0:T(8,128)}), f32[16,16,128]{2,1,0:T(8,128)S(1)}, u32[]{:S(2)}, u32[]{:S(2)}) async-start(f32[16,16,128]{2,1,0:T(8,128)} %broadcast_in_dim.103), calls=%async_computation | async-start | bytes 262144 | tf_op jit(solution)/shard_map/all_to_all | solution.py:33
  25.4 13.7 %all-to-all-done = f32[16,16,128]{2,1,0:T(8,128)S(1)} async-done(((f32[16,16,128]{2,1,0:T(8,128)}), f32[16,16,128]{2,1,0:T(8,128)S(1)}, u32[]{:S(2)}, u32[]{:S(2)}) %all-to-all-start) | async-done | bytes 131104 | tf_op jit(solution)/shard_map/all_to_all | solution.py:33
  39.1 2.6 stack.12
  41.7 4.6 all-to-all-start.1
  47.8 179.5 %all-to-all-done.1 = bf16[16,128,1024]{2,1,0:T(8,128)(2,1)} async-done(((bf16[16,128,1024]{2,1,0:T(8,128)(2,1)}), bf16[16,128,1024]{2,1,0:T(8,128)(2,1)}, u32[]{:S(2)}, u32[]{:S(2)}) %all-to-all-start.1) | async-done | bytes 4194336 | tf_op jit(solution)/shard_map/all_to_all | solution.py:71
  227.3 5.7 %multiply_convert_fusion = bf16[4,384,1024]{2,1,0:T(8,128)(2,1)} fusion(f32[4,384]{1,0:T(4,128)S(1)} %broadcast_in_dim.112, pred[1024]{0:T(1024)(128)(4,1)S(1)} %iota_compare_fusion.1, pred[4,384,512]{2,1,0:T(32,128)(4,1)S(1)} %bitcast_compare_fusion, bf16[4,512,1024]{2,1,0:T(8,128)(2,1)} %bitcast.7), kind=kOutput, calls=%fused_computation | convolution fusion | flops 1615331328 | bytes 8133632 | tf_op jit(solution)/shard_map/dot_general | solution.py:15
  233.0 7.7 %all-to-all-start.2 = ((bf16[32,48,1024]{2,1,0:T(8,128)(2,1)}), bf16[32,48,1024]{2,1,0:T(8,128)(2,1)S(1)}, u32[]{:S(2)}, u32[]{:S(2)}) async-start(bf16[32,48,1024]{2,1,0:T(8,128)(2,1)} %bitcast.213), calls=%async_computation.2 | async-start | bytes 6291456 | tf_op jit(solution)/shard_map/all_to_all | solution.py:82
  240.7 3.4 collective-permute-start.6
  244.1 4.6 collective-permute-start.7
  248.7 3.3 collective-permute-start.8
  252.1 2.5 collective-permute-start
  254.6 2.8 collective-permute-start.1
  263.8 23.5 %collective-permute-done.6 = bf16[512,384]{1,0:T(8,128)(2,1)} collective-permute-done((bf16[512,384]{1,0:T(8,128)(2,1)S(1)}, bf16[512,384]{1,0:T(8,128)(2,1)}, u32[]{:S(2)}, u32[]{:S(2)}) %collective-permute-start.6) | collective-permute-done | bytes 393248 | tf_op jit(solution)/shard_map/ppermute | solution.py:19
  287.2 4.4 collective-permute-start.2
  291.6 1.8 bitcast_dynamic-update-slice_fusion.2
  293.4 10.2 %collective-permute-done = bf16[384,512]{1,0:T(8,128)(2,1)} collective-permute-done((bf16[384,512]{1,0:T(8,128)(2,1)}, bf16[384,512]{1,0:T(8,128)(2,1)}, u32[]{:S(2)}, u32[]{:S(2)}) %collective-permute-start) | collective-permute-done | bytes 393248 | tf_op jit(solution)/shard_map/ppermute | solution.py:19
  303.6 2.4 collective-permute-start.3
  306.1 1.8 bitcast_dynamic-update-slice_fusion.8
  307.8 5.8 %collective-permute-start.4 = (bf16[512,384]{1,0:T(8,128)(2,1)S(1)}, bf16[512,384]{1,0:T(8,128)(2,1)S(1)}, u32[]{:S(2)}, u32[]{:S(2)}) collective-permute-start(bf16[512,384]{1,0:T(8,128)(2,1)S(1)} %bitcast.223), channel_id=1, source_target_pairs={{0,2},{1,3},{2,0},{3,1},{4,6},{5,7},{6,4},{7,5},{8,10},{9,11},{10,... | collective-permute-start | bytes 1179656 | tf_op jit(solution)/shard_map/ppermute | solution.py:19
  313.7 1.8 bitcast_dynamic-update-slice_fusion.1
  315.5 2.3 collective-permute-start.5
  317.8 1.8 bitcast_dynamic-update-slice_fusion.7
  319.5 1.8 bitcast_dynamic-update-slice_fusion
  323.6 7.2 %collective-permute-done.4 = bf16[512,384]{1,0:T(8,128)(2,1)S(1)} collective-permute-done((bf16[512,384]{1,0:T(8,128)(2,1)S(1)}, bf16[512,384]{1,0:T(8,128)(2,1)S(1)}, u32[]{:S(2)}, u32[]{:S(2)}) %collective-permute-start.4) | collective-permute-done | bytes 393248 | tf_op jit(solution)/shard_map/ppermute | solution.py:19
  347.6 2.3 multiply_convert_fusion.1
  349.9 1.5 fusion.46
  351.4 1.4 fusion.45
  352.8 1.4 fusion.44
  355.6 1.4 fusion.7
  357.0 1.4 fusion.8
  358.4 1.4 fusion.9
  359.8 1.4 fusion.10
  361.4 26.9 %all_to_all.20 = bf16[32,48,512]{2,1,0:T(8,128)(2,1)S(1)} all-to-all(bf16[32,48,512]{2,1,0:T(8,128)(2,1)S(1)} %bitcast.211), channel_id=1, replica_groups=mesh['z'=16,'y'=4,'c'=2,'x'=4] {'x','y','c'}, dimensions={0} | all-to-all | bytes 3145728 | tf_op jit(solution)/shard_map/all_to_all | solution.py:108
  388.3 2.6 convolution_convert_fusion
  391.8 3.2 collective-permute-start.11
  395.5 3.5 collective-permute-start.10
  399.4 3.2 collective-permute-start.17
  402.9 3.9 collective-permute-start.16
  407.3 1.9 collective-permute-start.15
  410.6 2.8 collective-permute-start.9
  413.9 1.6 collective-permute-done.17
  415.6 4.0 collective-permute-start.14
  419.6 11.3 %collective-permute-done.16 = bf16[384,512]{1,0:T(8,128)(2,1)S(1)} collective-permute-done((bf16[384,512]{1,0:T(8,128)(2,1)S(1)}, bf16[384,512]{1,0:T(8,128)(2,1)S(1)}, u32[]{:S(2)}, u32[]{:S(2)}) %collective-permute-start.16) | collective-permute-done | bytes 393248 | tf_op jit(solution)/shard_map/ppermute | solution.py:19
  430.9 4.4 collective-permute-start.13
  435.3 1.9 collective-permute-start.12
  440.9 6.6 %collective-permute-done.13 = bf16[512,384]{1,0:T(8,128)(2,1)S(1)} collective-permute-done((bf16[512,384]{1,0:T(8,128)(2,1)S(1)}, bf16[512,384]{1,0:T(8,128)(2,1)S(1)}, u32[]{:S(2)}, u32[]{:S(2)}) %collective-permute-start.13) | collective-permute-done | bytes 393248 | tf_op jit(solution)/shard_map/ppermute | solution.py:19
  447.5 1.8 collective-permute-done.12
  450.5 11.2 %reduce-scatter.2.cloned.1.call-done = bf16[128,512]{1,0:T(8,128)(2,1)} async-done(((bf16[2048,512]{1,0:T(8,128)(2,1)}), bf16[128,512]{1,0:T(8,128)(2,1)}) %reduce-scatter.2.cloned.1.call-update) | async-done | bytes 131088 | tf_op jit(solution)/shard_map/reduce_scatter | solution.py:112
  (84 shorter events, 40.4 us)
Async XLA Ops:
  9.2 29.9 %all-to-all-start = ((f32[16,16,128]{2,1,0:T(8,128)}), f32[16,16,128]{2,1,0:T(8,128)S(1)}, u32[]{:S(2)}, u32[]{:S(2)}) async-start(f32[16,16,128]{2,1,0:T(8,128)} %broadcast_in_dim.103), calls=%async_computation | async-start | bytes 262144 | tf_op jit(solution)/shard_map/all_to_all | solution.py:33
  41.7 185.6 %all-to-all-start.1 = ((bf16[16,128,1024]{2,1,0:T(8,128)(2,1)}), bf16[16,128,1024]{2,1,0:T(8,128)(2,1)}, u32[]{:S(2)}, u32[]{:S(2)}) async-start(bf16[16,128,1024]{2,1,0:T(8,128)(2,1)} %stack.12), calls=%async_computation.1 | async-start | bytes 8388608 | tf_op jit(solution)/shard_map/all_to_all | solution.py:71
  47.2 185.8 %copy-start.3 = (pred[4,384,512]{2,1,0:T(32,128)(4,1)}, pred[4,384,512]{2,1,0:T(32,128)(4,1)S(1)}, u32[]{:S(2)}) copy-start(pred[4,384,512]{2,1,0:T(32,128)(4,1)S(1)} %bitcast_compare_fusion) | copy-start | bytes 2359300
  233.0 7.7 %copy-start.5 = (bf16[1,512,384]{2,1,0:T(8,128)(2,1)S(1)}, bf16[1,512,384]{2,1,0:T(8,128)(2,1)}, u32[]{:S(2)}) copy-start(bf16[1,512,384]{2,1,0:T(8,128)(2,1)} %param.11) | copy-start | bytes 1179652
  233.0 99.5 %all-to-all-start.2 = ((bf16[32,48,1024]{2,1,0:T(8,128)(2,1)}), bf16[32,48,1024]{2,1,0:T(8,128)(2,1)S(1)}, u32[]{:S(2)}, u32[]{:S(2)}) async-start(bf16[32,48,1024]{2,1,0:T(8,128)(2,1)} %bitcast.213), calls=%async_computation.2 | async-start | bytes 6291456 | tf_op jit(solution)/shard_map/all_to_all | solution.py:82
  240.7 221.0 %reduce-scatter.2.cloned.1.call-start = ((), (), s32[]{:S(2)}) async-start(), calls=%async_computation.5 | async-start | bytes 2228224 | tf_op jit(solution)/shard_map/reduce_scatter | solution.py:112
  240.7 46.5 %collective-permute-start.6 = (bf16[512,384]{1,0:T(8,128)(2,1)S(1)}, bf16[512,384]{1,0:T(8,128)(2,1)}, u32[]{:S(2)}, u32[]{:S(2)}) collective-permute-start(bf16[512,384]{1,0:T(8,128)(2,1)S(1)} %bitcast.216), channel_id=1, source_target_pairs={{0,1},{1,2},{2,3},{3,0},{4,5},{5,6},{6,7},{7,4},{8,9},{9,10},{10,1... | collective-permute-start | bytes 1179656 | tf_op jit(solution)/shard_map/ppermute | solution.py:19
  244.1 63.7 %collective-permute-start.7 = (bf16[512,384]{1,0:T(8,128)(2,1)S(1)}, bf16[512,384]{1,0:T(8,128)(2,1)}, u32[]{:S(2)}, u32[]{:S(2)}) collective-permute-start(bf16[512,384]{1,0:T(8,128)(2,1)S(1)} %bitcast.217), channel_id=1, source_target_pairs={{0,2},{1,3},{2,0},{3,1},{4,6},{5,7},{6,4},{7,5},{8,10},{9,11},{10,... | collective-permute-start | bytes 1179656 | tf_op jit(solution)/shard_map/ppermute | solution.py:19
  248.7 70.8 %collective-permute-start.8 = (bf16[512,384]{1,0:T(8,128)(2,1)S(1)}, bf16[512,384]{1,0:T(8,128)(2,1)}, u32[]{:S(2)}, u32[]{:S(2)}) collective-permute-start(bf16[512,384]{1,0:T(8,128)(2,1)S(1)} %bitcast.218), channel_id=1, source_target_pairs={{0,3},{1,0},{2,1},{3,2},{4,7},{5,4},{6,5},{7,6},{8,11},{9,8},{10,9... | collective-permute-start | bytes 1179656 | tf_op jit(solution)/shard_map/ppermute | solution.py:19
  252.1 51.6 %collective-permute-start = (bf16[384,512]{1,0:T(8,128)(2,1)}, bf16[384,512]{1,0:T(8,128)(2,1)}, u32[]{:S(2)}, u32[]{:S(2)}) collective-permute-start(bf16[384,512]{1,0:T(8,128)(2,1)} %bitcast.219), channel_id=1, source_target_pairs={{0,1},{1,2},{2,3},{3,0},{4,5},{5,6},{6,7},{7,4},{8,9},{9,10},{10,1... | collective-permute-start | bytes 1179656 | tf_op jit(solution)/shard_map/ppermute | solution.py:19
  254.6 60.9 %collective-permute-start.1 = (bf16[384,512]{1,0:T(8,128)(2,1)}, bf16[384,512]{1,0:T(8,128)(2,1)}, u32[]{:S(2)}, u32[]{:S(2)}) collective-permute-start(bf16[384,512]{1,0:T(8,128)(2,1)} %bitcast.220), channel_id=1, source_target_pairs={{0,2},{1,3},{2,0},{3,1},{4,6},{5,7},{6,4},{7,5},{8,10},{9,11},{10,... | collective-permute-start | bytes 1179656 | tf_op jit(solution)/shard_map/ppermute | solution.py:19
  258.7 2.1 copy-start.6
  261.6 1.4 copy-start.8
  261.6 25.6 %copy-start.7 = (bf16[1,384,512]{2,1,0:T(8,128)(2,1)S(1)}, bf16[1,384,512]{2,1,0:T(8,128)(2,1)}, u32[]{:S(2)}) copy-start(bf16[1,384,512]{2,1,0:T(8,128)(2,1)} %param.13) | copy-start | bytes 1179652
  287.2 34.1 %collective-permute-start.2 = (bf16[384,512]{1,0:T(8,128)(2,1)S(1)}, bf16[384,512]{1,0:T(8,128)(2,1)S(1)}, u32[]{:S(2)}, u32[]{:S(2)}) collective-permute-start(bf16[384,512]{1,0:T(8,128)(2,1)S(1)} %bitcast.221), channel_id=1, source_target_pairs={{0,3},{1,0},{2,1},{3,2},{4,7},{5,4},{6,5},{7,6},{8,11},{9,8},{10,9... | collective-permute-start | bytes 1179656 | tf_op jit(solution)/shard_map/ppermute | solution.py:19
  303.6 19.1 %collective-permute-start.3 = (bf16[512,384]{1,0:T(8,128)(2,1)S(1)}, bf16[512,384]{1,0:T(8,128)(2,1)S(1)}, u32[]{:S(2)}, u32[]{:S(2)}) collective-permute-start(bf16[512,384]{1,0:T(8,128)(2,1)S(1)} %bitcast.222), channel_id=1, source_target_pairs={{0,1},{1,2},{2,3},{3,0},{4,5},{5,6},{6,7},{7,4},{8,9},{9,10},{10,1... | collective-permute-start | bytes 1179656 | tf_op jit(solution)/shard_map/ppermute | solution.py:19
  307.8 23.0 %collective-permute-start.4 = (bf16[512,384]{1,0:T(8,128)(2,1)S(1)}, bf16[512,384]{1,0:T(8,128)(2,1)S(1)}, u32[]{:S(2)}, u32[]{:S(2)}) collective-permute-start(bf16[512,384]{1,0:T(8,128)(2,1)S(1)} %bitcast.223), channel_id=1, source_target_pairs={{0,2},{1,3},{2,0},{3,1},{4,6},{5,7},{6,4},{7,5},{8,10},{9,11},{10,... | collective-permute-start | bytes 1179656 | tf_op jit(solution)/shard_map/ppermute | solution.py:19
  315.5 16.1 %collective-permute-start.5 = (bf16[512,384]{1,0:T(8,128)(2,1)S(1)}, bf16[512,384]{1,0:T(8,128)(2,1)S(1)}, u32[]{:S(2)}, u32[]{:S(2)}) collective-permute-start(bf16[512,384]{1,0:T(8,128)(2,1)S(1)} %bitcast.224), channel_id=1, source_target_pairs={{0,3},{1,0},{2,1},{3,2},{4,7},{5,4},{6,5},{7,6},{8,11},{9,8},{10,9... | collective-permute-start | bytes 1179656 | tf_op jit(solution)/shard_map/ppermute | solution.py:19
  349.9 4.3 copy-start
  361.4 26.9 %copy-start.4 = (pred[4,384,512]{2,1,0:T(32,128)(4,1)S(1)}, pred[4,384,512]{2,1,0:T(32,128)(4,1)}, u32[]{:S(2)}) copy-start(pred[4,384,512]{2,1,0:T(32,128)(4,1)} %copy-done.3) | copy-start | bytes 2359300
  391.3 7.6 %copy-start.2 = (bf16[384,384]{1,0:T(8,128)(2,1)S(1)}, bf16[384,384]{1,0:T(8,128)(2,1)}, u32[]{:S(2)}) copy-start(bf16[384,384]{1,0:T(8,128)(2,1)} %get-tuple-element.8) | copy-start | bytes 884740
  391.8 18.8 %collective-permute-start.11 = (bf16[512,384]{1,0:T(8,128)(2,1)S(1)}, bf16[512,384]{1,0:T(8,128)(2,1)S(1)}, u32[]{:S(2)}, u32[]{:S(2)}) collective-permute-start(bf16[512,384]{1,0:T(8,128)(2,1)S(1)} %convolution_convert_fusion.10), channel_id=1, source_target_pairs={{0,2},{1,3},{2,0},{3,1},{4,6},{5,7},{6,4},{7,5},{8,10},{9,11},{10,... | collective-permute-start | bytes 1179656 | tf_op jit(solution)/shard_map/ppermute | solution.py:19
  395.5 43.0 %collective-permute-start.10 = (bf16[512,384]{1,0:T(8,128)(2,1)S(1)}, bf16[512,384]{1,0:T(8,128)(2,1)S(1)}, u32[]{:S(2)}, u32[]{:S(2)}) collective-permute-start(bf16[512,384]{1,0:T(8,128)(2,1)S(1)} %convolution_convert_fusion.11), channel_id=1, source_target_pairs={{0,3},{1,0},{2,1},{3,2},{4,7},{5,4},{6,5},{7,6},{8,11},{9,8},{10,9... | collective-permute-start | bytes 1179656 | tf_op jit(solution)/shard_map/ppermute | solution.py:19
  399.3 10.3 %copy-start.1 = (bf16[384,384]{1,0:T(8,128)(2,1)S(1)}, bf16[384,384]{1,0:T(8,128)(2,1)}, u32[]{:S(2)}) copy-start(bf16[384,384]{1,0:T(8,128)(2,1)} %copy-done) | copy-start | bytes 884740
  399.4 16.2 %collective-permute-start.17 = (bf16[384,512]{1,0:T(8,128)(2,1)S(1)}, bf16[384,512]{1,0:T(8,128)(2,1)S(1)}, u32[]{:S(2)}, u32[]{:S(2)}) collective-permute-start(bf16[384,512]{1,0:T(8,128)(2,1)S(1)} %convolution_convert_fusion.2), channel_id=1, source_target_pairs={{0,2},{1,3},{2,0},{3,1},{4,6},{5,7},{6,4},{7,5},{8,10},{9,11},{10,... | collective-permute-start | bytes 1179656 | tf_op jit(solution)/shard_map/ppermute | solution.py:19
  402.9 28.0 %collective-permute-start.16 = (bf16[384,512]{1,0:T(8,128)(2,1)S(1)}, bf16[384,512]{1,0:T(8,128)(2,1)S(1)}, u32[]{:S(2)}, u32[]{:S(2)}) collective-permute-start(bf16[384,512]{1,0:T(8,128)(2,1)S(1)} %convolution_convert_fusion.3), channel_id=1, source_target_pairs={{0,3},{1,0},{2,1},{3,2},{4,7},{5,4},{6,5},{7,6},{8,11},{9,8},{10,9... | collective-permute-start | bytes 1179656 | tf_op jit(solution)/shard_map/ppermute | solution.py:19
  407.3 28.0 %collective-permute-start.15 = (bf16[384,512]{1,0:T(8,128)(2,1)S(1)}, bf16[384,512]{1,0:T(8,128)(2,1)S(1)}, u32[]{:S(2)}, u32[]{:S(2)}) collective-permute-start(bf16[384,512]{1,0:T(8,128)(2,1)S(1)} %convolution_convert_fusion.4), channel_id=1, source_target_pairs={{0,1},{1,2},{2,3},{3,0},{4,5},{5,6},{6,7},{7,4},{8,9},{9,10},{10,1... | collective-permute-start | bytes 1179656 | tf_op jit(solution)/shard_map/ppermute | solution.py:19
  410.6 27.8 %collective-permute-start.9 = (bf16[512,384]{1,0:T(8,128)(2,1)S(1)}, bf16[512,384]{1,0:T(8,128)(2,1)S(1)}, u32[]{:S(2)}, u32[]{:S(2)}) collective-permute-start(bf16[512,384]{1,0:T(8,128)(2,1)S(1)} %convolution_convert_fusion.12), channel_id=1, source_target_pairs={{0,1},{1,2},{2,3},{3,0},{4,5},{5,6},{6,7},{7,4},{8,9},{9,10},{10,1... | collective-permute-start | bytes 1179656 | tf_op jit(solution)/shard_map/ppermute | solution.py:19
  415.6 25.3 %collective-permute-start.14 = (bf16[512,384]{1,0:T(8,128)(2,1)S(1)}, bf16[512,384]{1,0:T(8,128)(2,1)S(1)}, u32[]{:S(2)}, u32[]{:S(2)}) collective-permute-start(bf16[512,384]{1,0:T(8,128)(2,1)S(1)} %convolution_convert_fusion.6), channel_id=1, source_target_pairs={{0,2},{1,3},{2,0},{3,1},{4,6},{5,7},{6,4},{7,5},{8,10},{9,11},{10,... | collective-permute-start | bytes 1179656 | tf_op jit(solution)/shard_map/ppermute | solution.py:19
  430.9 16.6 %collective-permute-start.13 = (bf16[512,384]{1,0:T(8,128)(2,1)S(1)}, bf16[512,384]{1,0:T(8,128)(2,1)S(1)}, u32[]{:S(2)}, u32[]{:S(2)}) collective-permute-start(bf16[512,384]{1,0:T(8,128)(2,1)S(1)} %convolution_convert_fusion.7), channel_id=1, source_target_pairs={{0,3},{1,0},{2,1},{3,2},{4,7},{5,4},{6,5},{7,6},{8,11},{9,8},{10,9... | collective-permute-start | bytes 1179656 | tf_op jit(solution)/shard_map/ppermute | solution.py:19
  435.3 13.9 %collective-permute-start.12 = (bf16[512,384]{1,0:T(8,128)(2,1)S(1)}, bf16[512,384]{1,0:T(8,128)(2,1)S(1)}, u32[]{:S(2)}, u32[]{:S(2)}) collective-permute-start(bf16[512,384]{1,0:T(8,128)(2,1)S(1)} %convolution_convert_fusion.8), channel_id=1, source_target_pairs={{0,1},{1,2},{2,3},{3,0},{4,5},{5,6},{6,7},{7,4},{8,9},{9,10},{10,1... | collective-permute-start | bytes 1179656 | tf_op jit(solution)/shard_map/ppermute | solution.py:19
Sparse Core Ops, SparseCore 0:
  391.1 70.5 reduce-scatter.1
